TPU v7x, 32 devices: a whole 2x2x4 slice. The times are simulated.
32 devices in a mesh: lat: 4 (over y, core), lon: 8 (over z, x).
Axes of the slice: x: 2, y: 2, z: 4, core: 2. Of those that a mesh axis runs over, the one named last changes fastest.
Arguments:
- cotangent: bfloat16 [4, 768, 32, 128], P('lat', 'lon'), may hold values from -6 to 6
- tiles: bfloat16 [64, 128, 128], replicated, may hold values from -0.25 to 0.25
- local_src: int32 [2, 4, 2304], P(None, 'lat', 'lon'), may hold values from 0 to 95
- local_tgt: int32 [2, 4, 2304], P(None, 'lat', 'lon'), may hold values from 0 to 95
- local_tile: int32 [2, 4, 2304], P(None, 'lat', 'lon'), may hold values from 0 to 63
- remote_src: int32 [2, 4, 2304], P(None, 'lat', 'lon'), may hold values from 0 to 95
- remote_tgt: int32 [2, 4, 2304], P(None, 'lat', 'lon'), may hold values from 0 to 95
- remote_tile: int32 [2, 4, 2304], P(None, 'lat', 'lon'), may hold values from 0 to 63
- remote_live: int32 [2, 4, 2304], P(None, 'lat', 'lon'), may hold values from 0 to 1, as said below
Outputs:
- initial_adjoint: float32 [4, 768, 32, 128], P('lat', 'lon')
Inputs may be any that keep to these rules, and one draw needn't show every extreme that they name: `remote_live`: A device's remote slots are laid out by owner sector p, then band offset d of 0 to 2, then k < 12; in each (p, d) cell the live slots come first; on every device the cell of the next sector east with d = 1 is full; and on a device (a, b) with 0 < a < 7, every cell whose owner sector p lies more than 4 sectors from b (counting around the circle) is empty.
All inputs are finite; a program needn't handle non-finite values.
Results may differ from a plain program's by a relative error of at most 0.0029.
Values may be sent and summed in bfloat16 or wider, within the bound.
A program may use at most 192 MiB of HBM per device.

v0:
```python
import jax
import jax.numpy as jnp
from jax import lax
from jax.sharding import PartitionSpec as P


def from_behind(value, axis, by):
    length = lax.axis_size(axis)
    pairs = [(i, i + by) for i in range(length) if 0 <= i + by < length]
    return lax.ppermute(value, axis, pairs)


def tile_products(gathered, tile_pick, tiles):
    return jnp.einsum(
        "ecj,eij->eci", gathered, tiles[tile_pick], preferred_element_type=jnp.float32
    )


def accumulate(block_count, values, dest_ids, weights):
    entry_count = values.shape[0]
    block_ids = lax.broadcasted_iota(jnp.int32, (block_count, entry_count), 0)
    selector = (block_ids == dest_ids[None, :]).astype(jnp.float32) * weights[None, :]
    flat = values.reshape(entry_count, -1)
    summed = jnp.dot(
        selector, flat, precision=lax.Precision.HIGHEST, preferred_element_type=jnp.float32
    )
    return summed.reshape((block_count,) + values.shape[1:])


def on_device(
    cotangent,
    tiles,
    local_src,
    local_tgt,
    local_tile,
    remote_src,
    remote_tgt,
    remote_tile,
    remote_live,
):
    band_index = lax.axis_index("lat")
    bands = lax.axis_size("lat")
    sectors = lax.axis_size("lon")
    south_cap = band_index == 0
    north_cap = band_index == bands - 1
    field = cotangent[0]
    blocks, channels, points = field.shape
    cells = (sectors, 3, remote_src.shape[2] // (sectors * 3))
    summed = jnp.zeros(field.shape, jnp.float32)
    for section in (1, 0):
        live = remote_live[section, 0]
        south_flag = south_cap.astype(jnp.float32)
        north_flag = north_cap.astype(jnp.float32)
        own_values = tile_products(field[local_tgt[section, 0]], local_tile[section, 0], tiles)
        outgoing = tile_products(field[remote_tgt[section, 0]], remote_tile[section, 0], tiles)
        outgoing = outgoing * live.astype(jnp.float32)[:, None, None]
        outgoing = outgoing.reshape(cells + (channels, points))
        owner_ids = remote_src[section, 0].reshape(cells)
        arrived, arrived_ids = (
            lax.all_to_all(outgoing, "lon", split_axis=0, concat_axis=0, tiled=True),
            lax.all_to_all(owner_ids, "lon", split_axis=0, concat_axis=0, tiled=True),
        )
        from_above, above_ids = from_behind((arrived[:, 0], arrived_ids[:, 0]), "lat", -1)
        from_below, below_ids = from_behind((arrived[:, 2], arrived_ids[:, 2]), "lat", 1)
        arrived_values = jnp.concatenate(
            [arrived[:, 1], from_above, from_below, arrived[:, 0], arrived[:, 2]], 0
        ).reshape(-1, channels, points)
        indices = jnp.concatenate(
            [arrived_ids[:, 1], above_ids, below_ids, arrived_ids[:, 0], arrived_ids[:, 2]], 0
        ).reshape(-1)
        unit = jnp.ones(arrived_ids[:, 1].shape, jnp.float32)
        flags = jnp.concatenate(
            [unit, unit, unit, unit * south_flag, unit * north_flag], 0
        ).reshape(-1)
        values = jnp.concatenate([own_values, arrived_values], 0)
        dest_ids = jnp.concatenate([local_src[section, 0], indices], 0)
        weights = jnp.concatenate([jnp.ones(local_src[section, 0].shape, jnp.float32), flags], 0)
        summed = accumulate(blocks, values, dest_ids, weights)
        if section == 1:
            field = summed.astype(jnp.bfloat16)
    return summed[None]


def solution(mesh):
    placed = (
        P("lat", "lon", None, None),
        P(),
        P(None, "lat", "lon"),
        P(None, "lat", "lon"),
        P(None, "lat", "lon"),
        P(None, "lat", "lon"),
        P(None, "lat", "lon"),
        P(None, "lat", "lon"),
        P(None, "lat", "lon"),
    )
    return jax.shard_map(
        on_device,
        mesh=mesh,
        in_specs=placed,
        out_specs=P("lat", "lon", None, None),
        check_vma=False,
    )
```

profile of v0, /device:TPU:5, one launch (start us, length us, event | category | flops | bytes accessed | tf_op | source)
XLA Modules:
  0.0 423.7 jit_solution(5620508194857265797)
XLA Ops:
  1.6 5.5 %all-to-all-start = ((s32[8,3,12]{2,1,0:T(4,128)}), s32[8,3,12]{2,1,0:T(4,128)S(1)}, u32[]{:S(2)}, u32[]{:S(2)}) async-start(s32[8,3,12]{2,1,0:T(4,128)} %reshape_squeeze.6), calls=%async_computation | async-start | bytes 32768 | tf_op jit(solution)/shard_map/all_to_all | solution.py:61
  13.6 10.4 %gather_fusion.3 = bf16[288,128,128]{2,1,0:T(8,128)(2,1)} fusion(bf16[64,128,128]{2,1,0:T(8,128)(2,1)S(1)} %copy-done, s32[1024]{0:T(1024)S(1)} %get-tuple-element.34), kind=kCustom, calls=%fused_computation.3 | custom fusion | bytes 18875520 | tf_op jit(solution)/shard_map/gather | solution.py:15
  23.9 11.6 %broadcast_multiply_fusion.1 = f32[288,32,128]{2,1,0:T(8,128)} fusion(f32[288]{0:T(512)S(1)} %get-tuple-element.17, bf16[288,32,128]{2,1,0:T(8,128)(2,1)} %gather_fusion.2, bf16[288,128,128]{2,1,0:T(8,128)(2,1)} %gather_fusion.3), kind=kOutput, calls=%fused_computation.13 | convolution fusion | flops 303169536 | bytes 16516224 | tf_op jit(solution)/shard_map/ecj,eij->eci/dot_general | solution.py:14
  35.5 5.9 %all-to-all-start.2 = ((f32[8,3,12,32,128]{4,3,2,1,0:T(8,128)}), f32[8,3,12,32,128]{4,3,2,1,0:T(8,128)}, u32[]{:S(2)}, u32[]{:S(2)}) async-start(f32[8,3,12,32,128]{4,3,2,1,0:T(8,128)} %bitcast.101), calls=%async_computation.2 | async-start | bytes 9437184 | tf_op jit(solution)/shard_map/all_to_all | solution.py:60
  44.5 10.4 %gather_fusion.1 = bf16[288,128,128]{2,1,0:T(8,128)(2,1)} fusion(bf16[64,128,128]{2,1,0:T(8,128)(2,1)S(1)} %copy-done, s32[1024]{0:T(1024)S(1)} %get-tuple-element.35), kind=kCustom, calls=%fused_computation.1 | custom fusion | bytes 18875520 | tf_op jit(solution)/shard_map/gather | solution.py:15
  54.8 11.6 %fusion.24 = f32[288,32,128]{2,1,0:T(8,128)} fusion(bf16[288,32,128]{2,1,0:T(8,128)(2,1)} %gather_fusion, bf16[288,128,128]{2,1,0:T(8,128)(2,1)} %gather_fusion.1), kind=kOutput, calls=%fused_computation.91 | convolution fusion | flops 301989888 | bytes 16515072 | tf_op jit(solution)/shard_map/ecj,eij->eci/dot_general | solution.py:14
  66.4 6.2 %copy.68 = f32[288,32,128]{0,2,1:T(8,128)} copy(f32[288,32,128]{2,1,0:T(8,128)} %fusion.24) | data formatting | bytes 9437184 | tf_op jit(solution)/shard_map/concatenate | solution.py:75
  73.7 10.4 %gather_fusion.7 = bf16[288,128,128]{2,1,0:T(8,128)(2,1)} fusion(bf16[64,128,128]{2,1,0:T(8,128)(2,1)S(1)} %copy-done, s32[1024]{0:T(1024)S(1)} %get-tuple-element.31), kind=kCustom, calls=%fused_computation.7 | custom fusion | bytes 18875520 | tf_op jit(solution)/shard_map/gather | solution.py:15
  88.8 55.6 %all-to-all-done.2 = f32[8,3,12,32,128]{4,3,2,1,0:T(8,128)} async-done(((f32[8,3,12,32,128]{4,3,2,1,0:T(8,128)}), f32[8,3,12,32,128]{4,3,2,1,0:T(8,128)}, u32[]{:S(2)}, u32[]{:S(2)}) %all-to-all-start.2) | async-done | bytes 4718624 | tf_op jit(solution)/shard_map/all_to_all | solution.py:60
  144.4 5.3 %all-to-all-start.1 = ((s32[8,3,12]{2,1,0:T(4,128)}), s32[8,3,12]{2,1,0:T(4,128)S(1)}, u32[]{:S(2)}, u32[]{:S(2)}) async-start(s32[8,3,12]{2,1,0:T(4,128)} %reshape_squeeze.7), calls=%async_computation.1 | async-start | bytes 32768 | tf_op jit(solution)/shard_map/all_to_all | solution.py:61
  173.5 10.7 %copy.79 = f32[60,8,32,128]{3,1,2,0:T(8,128)} copy(f32[60,8,32,128]{3,2,1,0:T(8,128)S(1)} %bitcast.103) | data formatting | bytes 15728640
  184.2 9.1 %copy.60 = f32[480,4096]{0,1:T(8,128)} copy(f32[480,4096]{1,0:T(8,128)} %bitcast.95) | data formatting | bytes 15728640 | tf_op jit(solution)/shard_map/concatenate | solution.py:75
  193.3 6.9 %pad_maximum_fusion = f32[768,4096]{0,1:T(8,128)S(1)} fusion(f32[480,4096]{0,1:T(8,128)} %copy.60, f32[288,4096]{0,1:T(8,128)} %bitcast.99), kind=kLoop, calls=%fused_computation.8 | loop fusion | flops 3145728 | bytes 25165824 | tf_op jit(solution)/shard_map/concatenate | solution.py:75
  200.2 12.1 %convolution_convert_fusion = bf16[96,32,128]{2,0,1:T(8,128)(2,1)S(1)} fusion(f32[32,128,768]{2,1,0:T(8,128)S(1)} %bitcast.94, s32[768]{0:T(1024)S(1)} %get-tuple-element.38, f32[768]{0:T(1024)S(1)} %concatenate.45), kind=kOutput, calls=%fused_computation.23 | convolution fusion | flops 3624419328 | bytes 13375488 | tf_op jit(solution)/shard_map/dot_general | solution.py:24
  215.6 8.0 %broadcast_multiply_fusion = f32[288,32,128]{2,1,0:T(8,128)S(1)} fusion(f32[288]{0:T(512)S(1)} %get-tuple-element.18, bf16[288,32,128]{2,1,0:T(8,128)(2,1)} %gather_fusion.6, bf16[288,128,128]{2,1,0:T(8,128)(2,1)} %gather_fusion.7), kind=kOutput, calls=%fused_computation.12 | convolution fusion | flops 303169536 | bytes 16516224 | tf_op jit(solution)/shard_map/ecj,eij->eci/dot_general | solution.py:14
  223.6 104.6 %all_to_all.20 = f32[8,3,12,32,128]{4,3,2,1,0:T(8,128)S(1)} all-to-all(f32[8,3,12,32,128]{4,3,2,1,0:T(8,128)S(1)} %bitcast.102), channel_id=1, replica_groups=mesh['lat'=4,'lon'=8] {'lon'}, dimensions={0} | all-to-all | bytes 9437184 | tf_op jit(solution)/shard_map/all_to_all | solution.py:60
  332.4 9.3 %collective-permute-start.6 = (f32[8,12,32,128]{3,2,1,0:T(8,128)}, f32[8,12,32,128]{3,2,1,0:T(8,128)}, u32[]{:S(2)}, u32[]{:S(2)}) collective-permute-start(f32[8,12,32,128]{3,2,1,0:T(8,128)} %get-tuple-element.20), channel_id=1, source_target_pairs={{8,0},{16,8},{24,16},{9,1},{17,9},{25,17},{10,2},{18,10},{26,18},{... | collective-permute-start | bytes 4718600 | tf_op jit(solution)/shard_map/ppermute | solution.py:10
  343.0 10.4 %gather_fusion.5 = bf16[288,128,128]{2,1,0:T(8,128)(2,1)} fusion(bf16[64,128,128]{2,1,0:T(8,128)(2,1)S(1)} %copy-done, s32[1024]{0:T(1024)S(1)} %get-tuple-element.32), kind=kCustom, calls=%fused_computation.5 | custom fusion | bytes 18875520 | tf_op jit(solution)/shard_map/gather | solution.py:15
  356.2 11.6 %fusion.25 = f32[288,32,128]{2,1,0:T(8,128)} fusion(bf16[288,32,128]{2,1,0:T(8,128)(2,1)} %gather_fusion.4, bf16[288,128,128]{2,1,0:T(8,128)(2,1)} %gather_fusion.5), kind=kOutput, calls=%fused_computation.92 | convolution fusion | flops 301989888 | bytes 16515072 | tf_op jit(solution)/shard_map/ecj,eij->eci/dot_general | solution.py:14
  367.9 6.6 %copy.69 = f32[288,32,128]{0,2,1:T(8,128)} copy(f32[288,32,128]{2,1,0:T(8,128)} %fusion.25) | data formatting | bytes 9437184 | tf_op jit(solution)/shard_map/concatenate | solution.py:75
  382.5 10.7 %copy.78 = f32[60,8,32,128]{3,1,2,0:T(8,128)} copy(f32[60,8,32,128]{3,2,1,0:T(8,128)S(1)} %bitcast.104) | data formatting | bytes 15728640
  393.2 9.0 %copy.66 = f32[480,4096]{0,1:T(8,128)} copy(f32[480,4096]{1,0:T(8,128)} %bitcast.96) | data formatting | bytes 15728640 | tf_op jit(solution)/shard_map/concatenate | solution.py:75
  402.2 7.1 %pad_maximum_fusion.1 = f32[768,4096]{0,1:T(8,128)S(1)} fusion(f32[480,4096]{0,1:T(8,128)} %copy.66, f32[288,4096]{0,1:T(8,128)} %bitcast.100), kind=kLoop, calls=%fused_computation.9 | loop fusion | flops 3145728 | bytes 25165824 | tf_op jit(solution)/shard_map/concatenate | solution.py:75
  409.3 12.2 %convolution_bitcast_fusion = f32[1,96,32,128]{3,1,2,0:T(8,128)S(1)} fusion(f32[32,128,768]{2,1,0:T(8,128)S(1)} %bitcast.93, f32[768]{0:T(1024)S(1)} %concatenate.45, s32[768]{0:T(1024)S(1)} %get-tuple-element.37), kind=kOutput, calls=%fused_computation.22 | convolution fusion | flops 3624026112 | bytes 14161920 | tf_op jit(solution)/shard_map/dot_general | solution.py:24
  (80 shorter events, 62.1 us)
Async XLA Ops:
  0.0 13.5 %copy-start = (bf16[64,128,128]{2,1,0:T(8,128)(2,1)S(1)}, bf16[64,128,128]{2,1,0:T(8,128)(2,1)}, u32[]{:S(2)}) copy-start(bf16[64,128,128]{2,1,0:T(8,128)(2,1)} %param.10) | copy-start | bytes 6291460
  1.6 33.9 %all-to-all-start = ((s32[8,3,12]{2,1,0:T(4,128)}), s32[8,3,12]{2,1,0:T(4,128)S(1)}, u32[]{:S(2)}, u32[]{:S(2)}) async-start(s32[8,3,12]{2,1,0:T(4,128)} %reshape_squeeze.6), calls=%async_computation | async-start | bytes 32768 | tf_op jit(solution)/shard_map/all_to_all | solution.py:61
  35.5 6.0 %copy-start.3 = (s32[2,1,288]{2,1,0:T(1,128)S(1)}, s32[2,1,288]{2,1,0:T(1,128)}, u32[]{:S(2)}) copy-start(s32[2,1,288]{2,1,0:T(1,128)} %param.13) | copy-start | bytes 6916
  35.5 6.0 %copy-start.2 = (bf16[1,96,32,128]{3,2,1,0:T(8,128)(2,1)S(1)}, bf16[1,96,32,128]{3,2,1,0:T(8,128)(2,1)}, u32[]{:S(2)}) copy-start(bf16[1,96,32,128]{3,2,1,0:T(8,128)(2,1)} %param.9) | copy-start | bytes 2359300
  35.5 109.0 %all-to-all-start.2 = ((f32[8,3,12,32,128]{4,3,2,1,0:T(8,128)}), f32[8,3,12,32,128]{4,3,2,1,0:T(8,128)}, u32[]{:S(2)}, u32[]{:S(2)}) async-start(f32[8,3,12,32,128]{4,3,2,1,0:T(8,128)} %bitcast.101), calls=%async_computation.2 | async-start | bytes 9437184 | tf_op jit(solution)/shard_map/all_to_all | solution.py:60
  73.7 10.4 %copy-start.4 = (s32[2,1,288]{2,1,0:T(1,128)S(1)}, s32[2,1,288]{2,1,0:T(1,128)}, u32[]{:S(2)}) copy-start(s32[2,1,288]{2,1,0:T(1,128)} %param.11) | copy-start | bytes 6916
  84.1 77.8 %collective-permute-start = (s32[8,12]{1,0:T(8,128)S(1)}, s32[8,12]{1,0:T(8,128)S(1)}, u32[]{:S(2)}, u32[]{:S(2)}) collective-permute-start(s32[8,12]{1,0:T(8,128)S(1)} %bitcast.107), channel_id=1, source_target_pairs={{8,0},{16,8},{24,16},{9,1},{17,9},{25,17},{10,2},{18,10},{26,18},{... | collective-permute-start | bytes 1160 | tf_op jit(solution)/shard_map/ppermute | solution.py:10
  87.5 76.2 %collective-permute-start.1 = (s32[8,12]{1,0:T(8,128)S(1)}, s32[8,12]{1,0:T(8,128)S(1)}, u32[]{:S(2)}, u32[]{:S(2)}) collective-permute-start(s32[8,12]{1,0:T(8,128)S(1)} %bitcast.105), channel_id=1, source_target_pairs={{0,8},{8,16},{16,24},{1,9},{9,17},{17,25},{2,10},{10,18},{18,26},{... | collective-permute-start | bytes 1160 | tf_op jit(solution)/shard_map/ppermute | solution.py:10
  144.4 13.1 %all-to-all-start.1 = ((s32[8,3,12]{2,1,0:T(4,128)}), s32[8,3,12]{2,1,0:T(4,128)S(1)}, u32[]{:S(2)}, u32[]{:S(2)}) async-start(s32[8,3,12]{2,1,0:T(4,128)} %reshape_squeeze.7), calls=%async_computation.1 | async-start | bytes 32768 | tf_op jit(solution)/shard_map/all_to_all | solution.py:61
  153.7 13.4 %collective-permute-start.4 = (f32[8,12,32,128]{3,2,1,0:T(8,128)}, f32[8,12,32,128]{3,2,1,0:T(8,128)}, u32[]{:S(2)}, u32[]{:S(2)}) collective-permute-start(f32[8,12,32,128]{3,2,1,0:T(8,128)} %get-tuple-element.22), channel_id=1, source_target_pairs={{8,0},{16,8},{24,16},{9,1},{17,9},{25,17},{10,2},{18,10},{26,18},{... | collective-permute-start | bytes 4718600 | tf_op jit(solution)/shard_map/ppermute | solution.py:10
  157.5 11.1 %collective-permute-start.5 = (f32[8,12,32,128]{3,2,1,0:T(8,128)}, f32[8,12,32,128]{3,2,1,0:T(8,128)}, u32[]{:S(2)}, u32[]{:S(2)}) collective-permute-start(f32[8,12,32,128]{3,2,1,0:T(8,128)} %get-tuple-element.21), channel_id=1, source_target_pairs={{0,8},{8,16},{16,24},{1,9},{9,17},{17,25},{2,10},{10,18},{18,26},{... | collective-permute-start | bytes 4718600 | tf_op jit(solution)/shard_map/ppermute | solution.py:10
  158.8 4.9 %collective-permute-start.2 = (s32[8,12]{1,0:T(8,128)S(1)}, s32[8,12]{1,0:T(8,128)S(1)}, u32[]{:S(2)}, u32[]{:S(2)}) collective-permute-start(s32[8,12]{1,0:T(8,128)S(1)} %bitcast.111), channel_id=1, source_target_pairs={{8,0},{16,8},{24,16},{9,1},{17,9},{25,17},{10,2},{18,10},{26,18},{... | collective-permute-start | bytes 1160 | tf_op jit(solution)/shard_map/ppermute | solution.py:10
  161.9 3.4 collective-permute-start.3
  328.2 2.2 copy-start.1
  332.4 43.7 %collective-permute-start.6 = (f32[8,12,32,128]{3,2,1,0:T(8,128)}, f32[8,12,32,128]{3,2,1,0:T(8,128)}, u32[]{:S(2)}, u32[]{:S(2)}) collective-permute-start(f32[8,12,32,128]{3,2,1,0:T(8,128)} %get-tuple-element.20), channel_id=1, source_target_pairs={{8,0},{16,8},{24,16},{9,1},{17,9},{25,17},{10,2},{18,10},{26,18},{... | collective-permute-start | bytes 4718600 | tf_op jit(solution)/shard_map/ppermute | solution.py:10
  341.7 36.0 %collective-permute-start.7 = (f32[8,12,32,128]{3,2,1,0:T(8,128)}, f32[8,12,32,128]{3,2,1,0:T(8,128)}, u32[]{:S(2)}, u32[]{:S(2)}) collective-permute-start(f32[8,12,32,128]{3,2,1,0:T(8,128)} %get-tuple-element.19), channel_id=1, source_target_pairs={{0,8},{8,16},{16,24},{1,9},{9,17},{17,25},{2,10},{10,18},{18,26},{... | collective-permute-start | bytes 4718600 | tf_op jit(solution)/shard_map/ppermute | solution.py:10
where the time goes:
time: 432 us; the launch traced here: 424 us
  local copies, waits for them, and re-layouts  135 us (31%)
  blocking collectives  105 us (24%)
  matrix products  67.1 us (16%)
  waiting for transfers between devices  57 us (13%)
  starting transfers between devices  41.9 us (10%)
  other arithmetic  17.1 us (4%)
    all_to_all x1, blocking collectives, on_device(): lax.all_to_all(outgoing, 'lon', split_axis=0, concat_axis=0, tiled=True)  105 us
    all_to_all x1, waiting for transfers between devices, on_device(): lax.all_to_all(outgoing, 'lon', split_axis=0, concat_axis=0, tiled=True)  55.6 us
    dot_general x4, matrix products, tile_products(): jnp.einsum('ecj,eij->eci', gathered, tiles[tile_pick], preferred_element_...  42.8 us
    gather x4, local copies, waits for them, and re-layouts, tile_products(): tiles[tile_pick]  41.5 us
    unnamed x28, local copies, waits for them, and re-layouts  36.4 us
    concatenate x4, local copies, waits for them, and re-layouts, on_device(): values = jnp.concatenate([own_values, arrived_values], 0)  30.9 us
    ppermute x8, starting transfers between devices, from_behind(): return lax.ppermute(value, axis, pairs)  25.2 us
    dot_general x2, matrix products, accumulate(): jnp.dot(selector, flat, precision=lax.Precision.HIGHEST, preferred_elemen...  24.3 us
  transfers between devices with their start and end apart: 11, of which 2 were waited for; matrix products, arithmetic and copies ran while one was open for 27% of the time, Pallas kernels for 0%

commit v1 on v0

v1 whole, which is shorter than its diff:
```python
import functools
import math

import jax
import jax.numpy as jnp
from jax import lax
from jax.experimental import pallas as pl
from jax.experimental.pallas import tpu as pltpu
from jax.sharding import PartitionSpec as P

MESH = pl.DeviceIdType.MESH
SHIFT = 7
MASK = (1 << SHIFT) - 1
LIMIT = 56 * 1024 * 1024


def product(block, tile):
    return lax.dot_general(
        block, tile, (((1,), (1,)), ((), ())), preferred_element_type=jnp.float32
    )


def exchange_kernel(
    bands,
    sectors,
    first,
    own_ref,
    far_tgt_ref,
    field_ref,
    tiles_ref,
    codes_ref,
    own_out,
    far_out,
    *rest,
):
    if first:
        codes_out, stage, recv, codes_in, codes, send_sem, recv_sem, code_send, code_recv, code_sem = rest
    else:
        stage, recv, send_sem, recv_sem = rest
        codes = codes_ref
    cells, cap = stage.shape[0], stage.shape[1]
    lane0 = 0 if first else cap
    band = lax.axis_index("lat")
    sector = lax.axis_index("lon")

    def offset_of(turn):
        turn_at = lax.div(turn + 1, 2)
        return sectors // 2 + turn_at * (1 - 2 * lax.rem(turn, 2))

    def out_cell(step):
        d = lax.rem(step, 3)
        to_sector = lax.rem(sector + offset_of(lax.div(step, 3)) + sectors, sectors)
        band_at = band + d - 1
        outside = jnp.logical_or(band_at < 0, band_at >= bands)
        to_band = jnp.where(outside, band, band_at)
        slot = jnp.where(outside, 2 - d, d)
        mine = jnp.logical_and(to_sector == sector, to_band == band)
        return to_sector * 3 + d, sector * 3 + slot, to_band, to_sector, mine

    def in_cell(step):
        slot = lax.rem(step, 3)
        of_sector = lax.rem(sector - offset_of(lax.div(step, 3)) + 2 * sectors, sectors)
        band_at = band + 1 - slot
        outside = jnp.logical_or(band_at < 0, band_at >= bands)
        of_band = jnp.where(outside, band, band_at)
        mine = jnp.logical_and(of_sector == sector, of_band == band)
        return of_sector * 3 + slot, mine

    barrier = pltpu.get_barrier_semaphore()

    def greet(step, carry):
        to_sector = lax.div(step, 3)
        to_band = band + lax.rem(step, 3) - 1
        inside = jnp.logical_and(to_band >= 0, to_band < bands)
        other = jnp.logical_not(jnp.logical_and(to_sector == sector, to_band == band))

        @pl.when(jnp.logical_and(inside, other))
        def _():
            pl.semaphore_signal(barrier, inc=1, device_id=(to_band, to_sector), device_id_type=MESH)

        return carry

    lax.fori_loop(0, cells, greet, 0)
    below = jnp.where(band > 0, 1, 0)
    above = jnp.where(band < bands - 1, 1, 0)
    pl.semaphore_wait(barrier, (1 + below + above) * sectors - 1)

    def data_copy(src, dst, to_band, to_sector):
        return pltpu.make_async_remote_copy(
            src_ref=stage.at[src],
            dst_ref=recv.at[dst],
            send_sem=send_sem.at[src],
            recv_sem=recv_sem.at[dst],
            device_id=(to_band, to_sector),
            device_id_type=MESH,
        )

    def code_copy(src, dst, to_band, to_sector):
        return pltpu.make_async_remote_copy(
            src_ref=codes_ref.at[src],
            dst_ref=codes_in.at[dst],
            send_sem=code_send.at[src],
            recv_sem=code_recv.at[dst],
            device_id=(to_band, to_sector),
            device_id_type=MESH,
        )

    def send(step, carry):
        src, dst, to_band, to_sector, mine = out_cell(step)
        if first:

            @pl.when(mine)
            def _():
                codes_in[dst] = codes_ref[src]

            @pl.when(jnp.logical_not(mine))
            def _():
                code_copy(src, dst, to_band, to_sector).start()

        for k in range(cap):
            stage[src, k] = field_ref[far_tgt_ref[src * cap + k]]

        @pl.when(mine)
        def _():
            recv[dst] = stage[src]

        @pl.when(jnp.logical_not(mine))
        def _():
            data_copy(src, dst, to_band, to_sector).start()

        return carry

    lax.fori_loop(0, cells, send, 0)

    own = own_ref.shape[0]
    group = math.gcd(own, 16)

    def own_products(step, carry):
        for k in range(group):
            at = step * group + k
            code = own_ref[at]
            own_out[at] = product(field_ref[code & MASK], tiles_ref[code >> SHIFT])
        return carry

    lax.fori_loop(0, own // group, own_products, 0)

    if first:

        def code_wait(step, carry):
            dst, mine = in_cell(step)

            @pl.when(jnp.logical_not(mine))
            def _():
                code_copy(dst, dst, band, sector).wait_recv()

            return carry

        lax.fori_loop(0, cells, code_wait, 0)
        local = pltpu.make_async_copy(codes_in, codes, code_sem)
        local.start()
        codes_out[...] = codes_in[...]
        local.wait()

    def far_products(step, carry):
        dst, mine = in_cell(step)

        @pl.when(jnp.logical_not(mine))
        def _():
            data_copy(dst, dst, band, sector).wait_recv()

        for k in range(cap):
            code = codes[dst, 0, lane0 + k]
            far_out[dst, k] = product(recv[dst, k], tiles_ref[code >> SHIFT])
        return carry

    lax.fori_loop(0, cells, far_products, 0)

    def drain(step, carry):
        src, dst, to_band, to_sector, mine = out_cell(step)

        @pl.when(jnp.logical_not(mine))
        def _():
            data_copy(src, dst, to_band, to_sector).wait_send()
            if first:
                code_copy(src, dst, to_band, to_sector).wait_send()

        return carry

    lax.fori_loop(0, cells, drain, 0)


def exchange(bands, sectors, first, own_codes, far_tgt, field, tiles, codes):
    cells = sectors * 3
    cap = far_tgt.shape[0] // cells
    block = field.shape[1:]
    smem = pl.BlockSpec(memory_space=pltpu.SMEM)
    vmem = pl.BlockSpec(memory_space=pltpu.VMEM)
    outs = [
        jax.ShapeDtypeStruct((own_codes.shape[0],) + block, jnp.float32),
        jax.ShapeDtypeStruct((cells, cap) + block, jnp.float32),
    ]
    scratch = [
        pltpu.VMEM((cells, cap) + block, jnp.bfloat16),
        pltpu.VMEM((cells, cap) + block, jnp.bfloat16),
    ]
    sems = [pltpu.SemaphoreType.DMA((cells,)), pltpu.SemaphoreType.DMA((cells,))]
    if first:
        outs.append(jax.ShapeDtypeStruct(codes.shape, jnp.int32))
        scratch += [pltpu.VMEM(codes.shape, jnp.int32), pltpu.SMEM(codes.shape, jnp.int32)]
        sems += [
            pltpu.SemaphoreType.DMA((cells,)),
            pltpu.SemaphoreType.DMA((cells,)),
            pltpu.SemaphoreType.DMA,
        ]
    entries = own_codes.shape[0] + far_tgt.shape[0]
    return pl.pallas_call(
        functools.partial(exchange_kernel, bands, sectors, first),
        out_shape=outs,
        in_specs=[smem, smem, vmem, vmem, vmem if first else smem],
        out_specs=[vmem] * len(outs),
        scratch_shapes=scratch + sems,
        compiler_params=pltpu.CompilerParams(
            collective_id=0 if first else 1, has_side_effects=True, vmem_limit_bytes=LIMIT
        ),
        cost_estimate=pl.CostEstimate(
            flops=2 * entries * block[0] * block[1] * block[1],
            bytes_accessed=entries * block[0] * block[1] * 8,
            transcendentals=0,
        ),
        name="exchange",
    )(own_codes, far_tgt, field, tiles, codes)


def gather_kernel(lane0, own_ref, codes_ref, own_values, far_values, out_ref, total):
    total[...] = jnp.zeros_like(total)
    own = own_ref.shape[0]
    group = math.gcd(own, 16)
    cells, cap = far_values.shape[0], far_values.shape[1]

    def own_add(step, carry):
        for k in range(group):
            at = step * group + k
            total[own_ref[at]] += own_values[at]
        return carry

    lax.fori_loop(0, own // group, own_add, 0)

    def far_add(cell, carry):
        for k in range(cap):
            total[codes_ref[cell, 0, lane0 + k] & MASK] += far_values[cell, k]
        return carry

    lax.fori_loop(0, cells, far_add, 0)
    out_ref[...] = total[0 : out_ref.shape[0]].astype(out_ref.dtype)


def gather(lane0, own_src, codes, own_values, far_values, blocks, kind):
    block = own_values.shape[1:]
    smem = pl.BlockSpec(memory_space=pltpu.SMEM)
    vmem = pl.BlockSpec(memory_space=pltpu.VMEM)
    return pl.pallas_call(
        functools.partial(gather_kernel, lane0),
        out_shape=jax.ShapeDtypeStruct((blocks,) + block, kind),
        in_specs=[smem, smem, vmem, vmem],
        out_specs=vmem,
        scratch_shapes=[pltpu.VMEM((blocks + 1,) + block, jnp.float32)],
        compiler_params=pltpu.CompilerParams(vmem_limit_bytes=LIMIT),
        name="gather",
    )(own_src, codes, own_values, far_values)


def on_device(
    bands,
    sectors,
    cotangent,
    tiles,
    local_src,
    local_tgt,
    local_tile,
    remote_src,
    remote_tgt,
    remote_tile,
    remote_live,
):
    field = cotangent[0]
    blocks = field.shape[0]
    cells = sectors * 3
    cap = remote_src.shape[2] // cells
    own_codes = local_tgt[:, 0] + (local_tile[:, 0] << SHIFT)
    source = jnp.where(remote_live[:, 0] > 0, remote_src[:, 0], blocks)
    far_codes = (source + (remote_tile[:, 0] << SHIFT)).reshape(2, cells, cap)
    codes = jnp.concatenate([far_codes[1], far_codes[0]], 1)
    codes = jnp.pad(codes, ((0, 0), (0, 128 - 2 * cap)))[:, None, :]
    for section in (1, 0):
        first = section == 1
        got = exchange(
            bands, sectors, first, own_codes[section], remote_tgt[section, 0], field, tiles, codes
        )
        if first:
            codes = got[2]
        field = gather(
            0 if first else cap,
            local_src[section, 0],
            codes,
            got[0],
            got[1],
            blocks,
            jnp.bfloat16 if first else jnp.float32,
        )
    return field[None]


def solution(mesh):
    placed = (P("lat", "lon", None, None), P()) + (P(None, "lat", "lon"),) * 7
    return jax.shard_map(
        functools.partial(on_device, mesh.shape["lat"], mesh.shape["lon"]),
        mesh=mesh,
        in_specs=placed,
        out_specs=P("lat", "lon", None, None),
        check_vma=False,
    )
```

time: 432 us -> 156 us (0.36)
  the two profiles are of different devices: /device:TPU:5 before, /device:TPU:21 now
where the time goes in v1:
time: 156 us; the launch traced here: 155 us
  Pallas kernels  150 us (96%)
  local copies, waits for them, and re-layouts  3.44 us (2%)
    pallas_call x2, Pallas kernels, exchange(): pl.pallas_call(functools.partial(exchange_kernel, bands, sectors, first),...  135 us
    pallas_call x2, Pallas kernels, gather(): pl.pallas_call(functools.partial(gather_kernel, lane0), out_shape=jax.Sha...  15.2 us

profile of v1, /device:TPU:21, one launch (start us, length us, event | category | flops | bytes accessed | tf_op | source)
XLA Modules:
  0.0 155.2 jit_solution(8130104327907720401)
XLA Ops:
  0.0 0.7 shift-left_add_fusion
  0.7 0.7 fusion
  1.5 1.3 slice_reduce_fusion.4
  2.8 1.3 slice_reduce_fusion
  4.1 0.1 squeeze.36
  4.2 0.1 squeeze.37
  4.3 0.1 pad_add_fusion
  4.3 0.6 pad.4
  5.0 70.0 %exchange.2 = (f32[288,32,128]{2,1,0:T(8,128)}, f32[24,12,32,128]{3,2,1,0:T(8,128)}, s32[24,1,128]{2,1,0:T(1,128)}) custom-call(s32[288]{0:T(512)} %get-tuple-element.20.own_ref, s32[288]{0:T(512)} %get-tuple-element.23.far_tgt_ref, bf16[96,32,128]{2,1,0:T(8,128)(2,1)} %bitcast.3, bf16[64,128,128]{2,1,0:T(8,128)(2,1)} %tiles_ref.3, s32[24,1,128]{2,1,0:T(1,128)} %bitcast.4), custom_call_target="tpu_custom_call" | custom-call | flops 603979776 | bytes 18874368 | tf_op jit(solution)/shard_map/exchange/pallas_call | solution.py:216
  75.0 7.7 %gather.2.field_ref = bf16[96,32,128]{2,1,0:T(8,128)(2,1)} custom-call(s32[288]{0:T(512)} %get-tuple-element.15.own_ref, s32[24,1,128]{2,1,0:T(1,128)} %get-tuple-element.10.codes_ref, f32[288,32,128]{2,1,0:T(8,128)} %get-tuple-element.11.own_values, f32[24,12,32,128]{3,2,1,0:T(8,128)} %get-tuple-element.12.far_values), custom_call_target="tpu_custom_call" | custom-call | tf_op jit(solution)/shard_map/gather/pallas_call | solution.py:261
  82.6 65.1 %exchange.3 = (f32[288,32,128]{2,1,0:T(8,128)}, f32[24,12,32,128]{3,2,1,0:T(8,128)}) custom-call(s32[288]{0:T(512)} %get-tuple-element.19.own_ref, s32[288]{0:T(512)} %get-tuple-element.24.far_tgt_ref, bf16[96,32,128]{2,1,0:T(8,128)(2,1)} %gather.2.field_ref, bf16[64,128,128]{2,1,0:T(8,128)(2,1)} %tiles_ref.3, s32[24,1,128]{2,1,0:T(1,128)} %get-tuple-element.10.codes_ref), custom_call_target="tpu_custom_call" | custom-call | flops 603979776 | bytes 18874368 | tf_op jit(solution)/shard_map/exchange/pallas_call | solution.py:216
  147.7 7.5 %gather.3 = f32[96,32,128]{2,1,0:T(8,128)} custom-call(s32[288]{0:T(512)} %get-tuple-element.16.own_ref, s32[24,1,128]{2,1,0:T(1,128)} %get-tuple-element.10.codes_ref, f32[288,32,128]{2,1,0:T(8,128)} %get-tuple-element.13.own_values, f32[24,12,32,128]{3,2,1,0:T(8,128)} %get-tuple-element.14.far_values), custom_call_target="tpu_custom_call" | custom-call | tf_op jit(solution)/shard_map/gather/pallas_call | solution.py:261
  (1 shorter events, 0.0 us)

commit v2 on v1

v2 whole, which is shorter than its diff:
```python
import functools
import math

import jax
import jax.numpy as jnp
from jax import lax
from jax.experimental import pallas as pl
from jax.experimental.pallas import tpu as pltpu
from jax.sharding import PartitionSpec as P

MESH = pl.DeviceIdType.MESH
SHIFT = 7
MASK = (1 << SHIFT) - 1
LIMIT = 56 * 1024 * 1024


def product(block, tile):
    return lax.dot_general(
        block, tile, (((1,), (1,)), ((), ())), preferred_element_type=jnp.float32
    )


def split(value):
    high = value.astype(jnp.bfloat16)
    return high, (value - high.astype(jnp.float32)).astype(jnp.bfloat16)


def steps_kernel(
    bands,
    sectors,
    own_ref,
    far_tgt_ref,
    own_src_ref,
    codes_ref,
    cotangent_ref,
    tiles_ref,
    out_ref,
    middle,
    stage,
    recv,
    codes_in,
    codes,
    own_values,
    far_values,
    picks,
    total,
    send_sem,
    recv_sem,
    code_send,
    code_recv,
    code_sem,
):
    cells, cap = stage.shape[0], stage.shape[1]
    blocks, channels, points = cotangent_ref.shape
    own = own_ref.shape[1]
    own_group = math.gcd(own, 16)
    rows = far_values.shape[0] // channels
    pad = rows // cells
    chunk = math.gcd(rows, 128)
    band = lax.axis_index("lat")
    sector = lax.axis_index("lon")

    def offset_of(turn):
        turn_at = lax.div(turn + 1, 2)
        return sectors // 2 + turn_at * (1 - 2 * lax.rem(turn, 2))

    def out_cell(step):
        d = lax.rem(step, 3)
        to_sector = lax.rem(sector + offset_of(lax.div(step, 3)) + sectors, sectors)
        band_at = band + d - 1
        outside = jnp.logical_or(band_at < 0, band_at >= bands)
        to_band = jnp.where(outside, band, band_at)
        slot = jnp.where(outside, 2 - d, d)
        mine = jnp.logical_and(to_sector == sector, to_band == band)
        return to_sector * 3 + d, sector * 3 + slot, to_band, to_sector, mine

    def in_cell(step):
        slot = lax.rem(step, 3)
        of_sector = lax.rem(sector - offset_of(lax.div(step, 3)) + 2 * sectors, sectors)
        band_at = band + 1 - slot
        outside = jnp.logical_or(band_at < 0, band_at >= bands)
        of_band = jnp.where(outside, band, band_at)
        mine = jnp.logical_and(of_sector == sector, of_band == band)
        return of_sector * 3 + slot, mine

    barrier = pltpu.get_barrier_semaphore()

    def greet(step, carry):
        to_sector = lax.div(step, 3)
        to_band = band + lax.rem(step, 3) - 1
        inside = jnp.logical_and(to_band >= 0, to_band < bands)
        other = jnp.logical_not(jnp.logical_and(to_sector == sector, to_band == band))

        @pl.when(jnp.logical_and(inside, other))
        def _():
            pl.semaphore_signal(barrier, inc=1, device_id=(to_band, to_sector), device_id_type=MESH)

        return carry

    lax.fori_loop(0, cells, greet, 0)
    below = jnp.where(band > 0, 1, 0)
    above = jnp.where(band < bands - 1, 1, 0)
    pl.semaphore_wait(barrier, (1 + below + above) * sectors - 1)

    def code_copy(src, dst, to_band, to_sector):
        return pltpu.make_async_remote_copy(
            src_ref=codes_ref.at[src],
            dst_ref=codes_in.at[dst],
            send_sem=code_send.at[src],
            recv_sem=code_recv.at[dst],
            device_id=(to_band, to_sector),
            device_id_type=MESH,
        )

    for turn, section in enumerate((1, 0)):
        first = turn == 0
        field_ref = cotangent_ref if first else middle

        def data_copy(src, dst, to_band, to_sector):
            return pltpu.make_async_remote_copy(
                src_ref=stage.at[src],
                dst_ref=recv.at[turn, dst],
                send_sem=send_sem.at[turn, src],
                recv_sem=recv_sem.at[turn, dst],
                device_id=(to_band, to_sector),
                device_id_type=MESH,
            )

        def send(step, carry):
            src, dst, to_band, to_sector, mine = out_cell(step)
            for k in range(cap):
                stage[src, k] = field_ref[far_tgt_ref[section, src * cap + k]]

            @pl.when(mine)
            def _():
                recv[turn, dst] = stage[src]
                if first:
                    codes_in[dst] = codes_ref[src]

            @pl.when(jnp.logical_not(mine))
            def _():
                if first:
                    code_copy(src, dst, to_band, to_sector).start()
                data_copy(src, dst, to_band, to_sector).start()

            return carry

        lax.fori_loop(0, cells, send, 0)

        if first:
            far_values[...] = jnp.zeros_like(far_values)

        def own_products(step, carry):
            for k in range(own_group):
                at = step * own_group + k
                code = own_ref[section, at]
                own_values[pl.ds(at, channels, stride=own), :] = product(
                    field_ref[code & MASK], tiles_ref[code >> SHIFT]
                )
            return carry

        lax.fori_loop(0, own // own_group, own_products, 0)

        block_ids = lax.broadcasted_iota(jnp.int32, (blocks, own), 0)
        own_pick = (block_ids == own_src_ref[section]).astype(jnp.float32).astype(jnp.bfloat16)

        def own_sum(c, carry):
            high, low = split(own_values[pl.ds(pl.multiple_of(c * own, 8), own), :])
            both = jnp.dot(
                own_pick,
                jnp.concatenate([high, low], 1),
                preferred_element_type=jnp.float32,
            )
            total[pl.ds(pl.multiple_of(c * blocks, 8), blocks), :] = (
                both[:, :points] + both[:, points:]
            )
            return carry

        lax.fori_loop(0, channels, own_sum, 0)

        if first:

            def code_wait(step, carry):
                dst, mine = in_cell(step)

                @pl.when(jnp.logical_not(mine))
                def _():
                    code_copy(dst, dst, band, sector).wait_recv()

                return carry

            lax.fori_loop(0, cells, code_wait, 0)
            local = pltpu.make_async_copy(codes_in, codes, code_sem)
            local.start()
            local.wait()

        row_ids = lax.broadcasted_iota(jnp.int32, (pad, points), 0)
        lane_ids = lax.broadcasted_iota(jnp.int32, (pad, points), 1)

        def far_products(step, carry):
            dst, mine = in_cell(step)

            @pl.when(jnp.logical_not(mine))
            def _():
                data_copy(dst, dst, band, sector).wait_recv()

            wanted = jnp.full((pad, points), -1, jnp.int32)
            for k in range(cap):
                code = codes[dst, 0, turn * cap + k]
                far_values[pl.ds(step * pad + k, channels, stride=rows), :] = product(
                    recv[turn, dst, k], tiles_ref[code >> SHIFT]
                )
                wanted = jnp.where(row_ids == k, code & MASK, wanted)
            picks[pl.ds(pl.multiple_of(step * pad, pad), pad), :] = (wanted == lane_ids).astype(
                jnp.float32
            )
            return carry

        per_chunk = chunk // pad
        for part in range(rows // chunk):
            lax.fori_loop(part * per_chunk, (part + 1) * per_chunk, far_products, 0)
            pick = picks[part * chunk : (part + 1) * chunk, :].T[:blocks].astype(jnp.bfloat16)
            pick = jnp.concatenate([pick, pick], 1)

            def far_sum(pair, carry):
                parts = []
                for c in range(2):
                    at = pl.multiple_of((pair * 2 + c) * rows + part * chunk, 8)
                    parts.append(jnp.concatenate(split(far_values[pl.ds(at, chunk), :]), 0))
                both = jnp.dot(
                    pick, jnp.concatenate(parts, 1), preferred_element_type=jnp.float32
                )
                for c in range(2):
                    at = pl.multiple_of((pair * 2 + c) * blocks, 8)
                    total[pl.ds(at, blocks), :] += both[:, c * points : (c + 1) * points]
                return carry

            lax.fori_loop(0, channels // 2, far_sum, 0, unroll=4)

        def drain(step, carry):
            src, dst, to_band, to_sector, mine = out_cell(step)

            @pl.when(jnp.logical_not(mine))
            def _():
                data_copy(src, dst, to_band, to_sector).wait_send()
                if first:
                    code_copy(src, dst, to_band, to_sector).wait_send()

            return carry

        lax.fori_loop(0, cells, drain, 0)

        def finish(step, carry):
            for k in range(8):
                n = step * 8 + k
                value = total[pl.ds(n, channels, stride=blocks), :]
                if first:
                    middle[n] = value.astype(jnp.bfloat16)
                else:
                    out_ref[n] = value
            return carry

        lax.fori_loop(0, blocks // 8, finish, 0)


def both_steps(bands, sectors, own_codes, far_tgt, own_src, codes, field, tiles):
    cells = sectors * 3
    cap = far_tgt.shape[1] // cells
    pad = (cap + 15) // 16 * 16
    blocks, channels, points = field.shape
    own = own_codes.shape[1]
    smem = pl.BlockSpec(memory_space=pltpu.SMEM)
    vmem = pl.BlockSpec(memory_space=pltpu.VMEM)
    dma = pltpu.SemaphoreType.DMA
    entries = 2 * (own + far_tgt.shape[1])
    return pl.pallas_call(
        functools.partial(steps_kernel, bands, sectors),
        out_shape=jax.ShapeDtypeStruct(field.shape, jnp.float32),
        in_specs=[smem, smem, vmem, vmem, vmem, vmem],
        out_specs=vmem,
        scratch_shapes=[
            pltpu.VMEM(field.shape, jnp.bfloat16),
            pltpu.VMEM((cells, cap, channels, points), jnp.bfloat16),
            pltpu.VMEM((2, cells, cap, channels, points), jnp.bfloat16),
            pltpu.VMEM(codes.shape, jnp.int32),
            pltpu.SMEM(codes.shape, jnp.int32),
            pltpu.VMEM((channels * own, points), jnp.float32),
            pltpu.VMEM((channels * cells * pad, points), jnp.float32),
            pltpu.VMEM((cells * pad, points), jnp.float32),
            pltpu.VMEM((channels * blocks, points), jnp.float32),
            dma((2, cells)),
            dma((2, cells)),
            dma((cells,)),
            dma((cells,)),
            dma,
        ],
        compiler_params=pltpu.CompilerParams(
            collective_id=0, has_side_effects=True, vmem_limit_bytes=LIMIT
        ),
        cost_estimate=pl.CostEstimate(
            flops=2 * entries * channels * points * points,
            bytes_accessed=entries * channels * points * 8,
            transcendentals=0,
        ),
        name="both_steps",
    )(own_codes, far_tgt, own_src, codes, field, tiles)


def on_device(
    bands,
    sectors,
    cotangent,
    tiles,
    local_src,
    local_tgt,
    local_tile,
    remote_src,
    remote_tgt,
    remote_tile,
    remote_live,
):
    field = cotangent[0]
    blocks = field.shape[0]
    cells = sectors * 3
    cap = remote_src.shape[2] // cells
    own_codes = local_tgt[:, 0] + (local_tile[:, 0] << SHIFT)
    source = jnp.where(remote_live[:, 0] > 0, remote_src[:, 0], blocks)
    far_codes = (source + (remote_tile[:, 0] << SHIFT)).reshape(2, cells, cap)
    codes = jnp.concatenate([far_codes[1], far_codes[0]], 1)
    codes = jnp.pad(codes, ((0, 0), (0, 128 - 2 * cap)))[:, None, :]
    summed = both_steps(
        bands, sectors, own_codes, remote_tgt[:, 0], local_src, codes, field, tiles
    )
    return summed[None]


def solution(mesh):
    placed = (P("lat", "lon", None, None), P()) + (P(None, "lat", "lon"),) * 7
    return jax.shard_map(
        functools.partial(on_device, mesh.shape["lat"], mesh.shape["lon"]),
        mesh=mesh,
        in_specs=placed,
        out_specs=P("lat", "lon", None, None),
        check_vma=False,
    )
```

time: 156 us -> 131 us (0.84)
  the two profiles are of different devices: /device:TPU:21 before, /device:TPU:15 now
where the time goes in v2:
time: 131 us
  Pallas kernels  126 us (96%)
  local copies, waits for them, and re-layouts  3.49 us (3%)
  other arithmetic  2.1 us (2%)
    pallas_call x1, Pallas kernels, both_steps(): pl.pallas_call(functools.partial(steps_kernel, bands, sectors), out_shape...  126 us
    unnamed x1, local copies, waits for them, and re-layouts  2.67 us

profile of v2, /device:TPU:15, one launch (start us, length us, event | category | flops | bytes accessed | tf_op | source)
XLA Modules:
  0.0 131.2 jit_solution(10053698249662517810)
XLA Ops:
  0.0 0.7 fusion
  0.7 1.3 copy_bitcast_fusion
  2.1 0.1 squeeze.18
  2.1 0.1 squeeze.19
  2.2 0.1 pad_add_fusion
  2.3 0.6 pad.4
  2.9 125.6 %both_steps.1 = f32[96,32,128]{2,1,0:T(8,128)} custom-call(s32[2,288]{1,0:T(2,128)} %get-tuple-element.8.own_ref, s32[2,288]{1,0:T(2,128)} %get-tuple-element.7.far_tgt_ref, s32[2,1,288]{2,1,0:T(1,128)} %own_src_ref.1, s32[24,1,128]{2,1,0:T(1,128)} %bitcast.9, bf16[96,32,128]{2,1,0:T(8,128)(2,1)} %bitcast.8, bf16[64,128,128]{2,1,0:T(8,128)(2,1)} %tiles_ref.1), custom_call_target="tpu_custom_call" | custom-call | flops 1207959552 | bytes 37748736 | tf_op jit(solution)/shard_map/both_steps/pallas_call | solution.py:276
  128.6 2.7 %copy.34 = f32[1,96,32,128]{3,2,1,0:T(8,128)} copy(f32[1,96,32,128]{3,2,1,0:T(8,128)} %bitcast.7) | data formatting | bytes 3145728
  (1 shorter events, 0.0 us)

commit v3 on v2

--- a/solution.py
+++ b/solution.py
@@ -32,6 +32,7 @@
     far_tgt_ref,
     own_src_ref,
     codes_ref,
+    targets_ref,
     cotangent_ref,
     tiles_ref,
     out_ref,
@@ -40,6 +41,10 @@
     recv,
     codes_in,
     codes,
+    passing_first,
+    passing_second,
+    targets_in,
+    targets,
     own_values,
     far_values,
     picks,
@@ -49,6 +54,10 @@
     code_send,
     code_recv,
     code_sem,
+    field_send,
+    field_recv,
+    target_send,
+    target_recv,
 ):
     cells, cap = stage.shape[0], stage.shape[1]
     blocks, channels, points = cotangent_ref.shape
@@ -60,27 +69,47 @@
     band = lax.axis_index("lat")
     sector = lax.axis_index("lon")
 
-    def offset_of(turn):
-        turn_at = lax.div(turn + 1, 2)
-        return sectors // 2 + turn_at * (1 - 2 * lax.rem(turn, 2))
-
-    def out_cell(step):
-        d = lax.rem(step, 3)
-        to_sector = lax.rem(sector + offset_of(lax.div(step, 3)) + sectors, sectors)
+    half = sectors // 2
+    near_steps = 3 * half
+    base = lax.div(sector, half) * half
+    other_base = half - base
+    partner = lax.rem(sector + half, sectors)
+    relays = lax.rem(band, 2) == 0
+
+    def landing(d, to_sector):
         band_at = band + d - 1
         outside = jnp.logical_or(band_at < 0, band_at >= bands)
         to_band = jnp.where(outside, band, band_at)
         slot = jnp.where(outside, 2 - d, d)
         mine = jnp.logical_and(to_sector == sector, to_band == band)
-        return to_sector * 3 + d, sector * 3 + slot, to_band, to_sector, mine
+        return slot, to_band, mine
+
+    def origin(slot):
+        band_at = band + 1 - slot
+        outside = jnp.logical_or(band_at < 0, band_at >= bands)
+        return jnp.where(outside, band, band_at)
+
+    def out_cell(step):
+        d = lax.rem(step, 3)
+        near = base + lax.rem(sector + lax.div(step, 3), half)
+        far = other_base + lax.rem(sector + lax.div(step, 3), half)
+        crosses = step >= near_steps
+        passes_on = jnp.logical_and(crosses, relays)
+        to_sector = jnp.where(jnp.logical_and(crosses, jnp.logical_not(relays)), far, near)
+        held = jnp.where(crosses, far, near)
+        of_sector = jnp.where(passes_on, partner, sector)
+        slot, to_band, mine = landing(d, to_sector)
+        return held * 3 + d, to_sector * 3 + d, of_sector * 3 + slot, to_band, to_sector, mine
 
     def in_cell(step):
         slot = lax.rem(step, 3)
-        of_sector = lax.rem(sector - offset_of(lax.div(step, 3)) + 2 * sectors, sectors)
-        band_at = band + 1 - slot
-        outside = jnp.logical_or(band_at < 0, band_at >= bands)
-        of_band = jnp.where(outside, band, band_at)
-        mine = jnp.logical_and(of_sector == sector, of_band == band)
+        turned = lax.rem(sector - lax.div(step, 3) + 2 * sectors, half)
+        crosses = step >= near_steps
+        of_sector = jnp.where(crosses, other_base, base) + turned
+        of_band = origin(slot)
+        passed_on = jnp.logical_and(crosses, lax.rem(of_band, 2) == 0)
+        via = jnp.where(passed_on, lax.rem(of_sector + half, sectors), of_sector)
+        mine = jnp.logical_and(via == sector, of_band == band)
         return of_sector * 3 + slot, mine
 
     barrier = pltpu.get_barrier_semaphore()
@@ -112,9 +141,56 @@
             device_id_type=MESH,
         )
 
+    def target_copy():
+        return pltpu.make_async_remote_copy(
+            src_ref=targets_ref,
+            dst_ref=targets_in,
+            send_sem=target_send,
+            recv_sem=target_recv,
+            device_id=(band, partner),
+            device_id_type=MESH,
+        )
+
+    def code_out(cell):
+        to_sector = lax.div(cell, 3)
+        slot, to_band, mine = landing(lax.rem(cell, 3), to_sector)
+        return code_copy(cell, sector * 3 + slot, to_band, to_sector), sector * 3 + slot, mine
+
+    def send_codes(cell, carry):
+        copy, dst, mine = code_out(cell)
+
+        @pl.when(mine)
+        def _():
+            codes_in[dst] = codes_ref[cell]
+
+        @pl.when(jnp.logical_not(mine))
+        def _():
+            copy.start()
+
+        return carry
+
+    def wait_codes(cell, carry):
+        mine = jnp.logical_and(lax.div(cell, 3) == sector, origin(lax.rem(cell, 3)) == band)
+
+        @pl.when(jnp.logical_not(mine))
+        def _():
+            code_copy(cell, cell, band, sector).wait_recv()
+
+        return carry
+
+    def drain_codes(cell, carry):
+        copy, _, mine = code_out(cell)
+
+        @pl.when(jnp.logical_not(mine))
+        def _():
+            copy.wait_send()
+
+        return carry
+
     for turn, section in enumerate((1, 0)):
         first = turn == 0
         field_ref = cotangent_ref if first else middle
+        passing = passing_first if first else passing_second
 
         def data_copy(src, dst, to_band, to_sector):
             return pltpu.make_async_remote_copy(
@@ -126,26 +202,47 @@
                 device_id_type=MESH,
             )
 
-        def send(step, carry):
-            src, dst, to_band, to_sector, mine = out_cell(step)
+        def field_copy():
+            return pltpu.make_async_remote_copy(
+                src_ref=field_ref,
+                dst_ref=passing,
+                send_sem=field_send.at[turn],
+                recv_sem=field_recv.at[turn],
+                device_id=(band, partner),
+                device_id_type=MESH,
+            )
+
+        def put(step, blocks_ref, pick_target):
+            held, listed, dst, to_band, to_sector, mine = out_cell(step)
             for k in range(cap):
-                stage[src, k] = field_ref[far_tgt_ref[section, src * cap + k]]
+                stage[held, k] = blocks_ref[pick_target(listed * cap + k)]
 
             @pl.when(mine)
             def _():
-                recv[turn, dst] = stage[src]
-                if first:
-                    codes_in[dst] = codes_ref[src]
+                recv[turn, dst] = stage[held]
 
             @pl.when(jnp.logical_not(mine))
             def _():
-                if first:
-                    code_copy(src, dst, to_band, to_sector).start()
-                data_copy(src, dst, to_band, to_sector).start()
-
-            return carry
-
-        lax.fori_loop(0, cells, send, 0)
+                data_copy(held, dst, to_band, to_sector).start()
+
+        def send(step, carry):
+            put(step, field_ref, lambda at: far_tgt_ref[section, at])
+            return carry
+
+        def pass_on(step, carry):
+            put(step, passing, lambda at: targets[section, 0, at])
+            return carry
+
+        @pl.when(relays)
+        def _():
+            field_copy().start()
+            if first:
+                target_copy().start()
+
+        lax.fori_loop(0, near_steps, send, 0)
+
+        if first:
+            lax.fori_loop(0, cells, send_codes, 0)
 
         if first:
             far_values[...] = jnp.zeros_like(far_values)
@@ -178,18 +275,13 @@
 
         lax.fori_loop(0, channels, own_sum, 0)
 
+        @pl.when(jnp.logical_not(relays))
+        def _():
+            lax.fori_loop(near_steps, cells, send, 0)
+
+
         if first:
-
-            def code_wait(step, carry):
-                dst, mine = in_cell(step)
-
-                @pl.when(jnp.logical_not(mine))
-                def _():
-                    code_copy(dst, dst, band, sector).wait_recv()
-
-                return carry
-
-            lax.fori_loop(0, cells, code_wait, 0)
+            lax.fori_loop(0, cells, wait_codes, 0)
             local = pltpu.make_async_copy(codes_in, codes, code_sem)
             local.start()
             local.wait()
@@ -217,7 +309,20 @@
             return carry
 
         per_chunk = chunk // pad
+        relay_part = near_steps // per_chunk
         for part in range(rows // chunk):
+            if part == relay_part:
+
+                @pl.when(relays)
+                def _():
+                    if first:
+                        target_copy().wait_recv()
+                        listed = pltpu.make_async_copy(targets_in, targets, code_sem)
+                        listed.start()
+                        listed.wait()
+                    field_copy().wait_recv()
+                    lax.fori_loop(near_steps, cells, pass_on, 0)
+
             lax.fori_loop(part * per_chunk, (part + 1) * per_chunk, far_products, 0)
             pick = picks[part * chunk : (part + 1) * chunk, :].T[:blocks].astype(jnp.bfloat16)
             pick = jnp.concatenate([pick, pick], 1)
@@ -238,17 +343,24 @@
             lax.fori_loop(0, channels // 2, far_sum, 0, unroll=4)
 
         def drain(step, carry):
-            src, dst, to_band, to_sector, mine = out_cell(step)
+            held, _, dst, to_band, to_sector, mine = out_cell(step)
 
             @pl.when(jnp.logical_not(mine))
             def _():
-                data_copy(src, dst, to_band, to_sector).wait_send()
-                if first:
-                    code_copy(src, dst, to_band, to_sector).wait_send()
+                data_copy(held, dst, to_band, to_sector).wait_send()
 
             return carry
 
         lax.fori_loop(0, cells, drain, 0)
+
+        @pl.when(relays)
+        def _():
+            field_copy().wait_send()
+            if first:
+                target_copy().wait_send()
+
+        if first:
+            lax.fori_loop(0, cells, drain_codes, 0)
 
         def finish(step, carry):
             for k in range(8):
@@ -263,7 +375,8 @@
         lax.fori_loop(0, blocks // 8, finish, 0)
 
 
-def both_steps(bands, sectors, own_codes, far_tgt, own_src, codes, field, tiles):
+def both_steps(bands, sectors, own_codes, targets, own_src, codes, field, tiles):
+    far_tgt = targets[:, 0]
     cells = sectors * 3
     cap = far_tgt.shape[1] // cells
     pad = (cap + 15) // 16 * 16
@@ -276,7 +389,7 @@
     return pl.pallas_call(
         functools.partial(steps_kernel, bands, sectors),
         out_shape=jax.ShapeDtypeStruct(field.shape, jnp.float32),
-        in_specs=[smem, smem, vmem, vmem, vmem, vmem],
+        in_specs=[smem, smem, vmem, vmem, vmem, vmem, vmem],
         out_specs=vmem,
         scratch_shapes=[
             pltpu.VMEM(field.shape, jnp.bfloat16),
@@ -284,6 +397,10 @@
             pltpu.VMEM((2, cells, cap, channels, points), jnp.bfloat16),
             pltpu.VMEM(codes.shape, jnp.int32),
             pltpu.SMEM(codes.shape, jnp.int32),
+            pltpu.VMEM(field.shape, jnp.bfloat16),
+            pltpu.VMEM(field.shape, jnp.bfloat16),
+            pltpu.VMEM(targets.shape, jnp.int32),
+            pltpu.SMEM(targets.shape, jnp.int32),
             pltpu.VMEM((channels * own, points), jnp.float32),
             pltpu.VMEM((channels * cells * pad, points), jnp.float32),
             pltpu.VMEM((cells * pad, points), jnp.float32),
@@ -292,6 +409,10 @@
             dma((2, cells)),
             dma((cells,)),
             dma((cells,)),
+            dma,
+            dma((2,)),
+            dma((2,)),
+            dma,
             dma,
         ],
         compiler_params=pltpu.CompilerParams(
@@ -303,7 +424,7 @@
             transcendentals=0,
         ),
         name="both_steps",
-    )(own_codes, far_tgt, own_src, codes, field, tiles)
+    )(own_codes, far_tgt, own_src, codes, targets, field, tiles)
 
 
 def on_device(
@@ -329,7 +450,7 @@
     codes = jnp.concatenate([far_codes[1], far_codes[0]], 1)
     codes = jnp.pad(codes, ((0, 0), (0, 128 - 2 * cap)))[:, None, :]
     summed = both_steps(
-        bands, sectors, own_codes, remote_tgt[:, 0], local_src, codes, field, tiles
+        bands, sectors, own_codes, remote_tgt, local_src, codes, field, tiles
     )
     return summed[None]
 

time: 131 us -> 115 us (0.88)
  the two profiles are of different devices: /device:TPU:15 before, /device:TPU:5 now
where the time goes in v3:
time: 115 us
  Pallas kernels  109 us (95%)
  local copies, waits for them, and re-layouts  3.49 us (3%)
  other arithmetic  2.1 us (2%)
    pallas_call x1, Pallas kernels, both_steps(): pl.pallas_call(functools.partial(steps_kernel, bands, sectors), out_shape...  109 us
    unnamed x1, local copies, waits for them, and re-layouts  2.67 us

profile of v3, /device:TPU:5, one launch (start us, length us, event | category | flops | bytes accessed | tf_op | source)
XLA Modules:
  0.0 115.0 jit_solution(7211613950497286006)
XLA Ops:
  0.0 0.7 fusion
  0.7 1.3 %copy_bitcast_fusion = (s32[2,288]{1,0:T(2,128)}, s32[2,288]{1,0:T(2,128)}) fusion(s32[2,1,288]{2,1,0:T(1,128)} %targets_ref.1, s32[2,1,288]{2,1,0:T(1,128)} %param.13, s32[2,1,288]{2,1,0:T(1,128)} %param.12), kind=kLoop, calls=%fused_computation.3 | loop fusion | flops 1152 | bytes 11520
  2.1 0.1 squeeze.18
  2.1 0.1 squeeze.19
  2.2 0.1 pad_add_fusion
  2.3 0.6 pad.4
  2.9 109.4 %both_steps.1 = f32[96,32,128]{2,1,0:T(8,128)} custom-call(s32[2,288]{1,0:T(2,128)} %get-tuple-element.8.own_ref, s32[2,288]{1,0:T(2,128)} %get-tuple-element.7.far_tgt_ref, s32[2,1,288]{2,1,0:T(1,128)} %own_src_ref.1, s32[24,1,128]{2,1,0:T(1,128)} %bitcast.9, s32[2,1,288]{2,1,0:T(1,128)} %targets_ref.1, bf16[96,32,128]{2,1,0:T(8,128)(2,1)} %bitcast.8, ...), custom_call_target="tpu_custom_call" | custom-call | flops 1207959552 | bytes 37748736 | tf_op jit(solution)/shard_map/both_steps/pallas_call | solution.py:389
  112.3 2.7 %copy.34 = f32[1,96,32,128]{3,2,1,0:T(8,128)} copy(f32[1,96,32,128]{3,2,1,0:T(8,128)} %bitcast.7) | data formatting | bytes 3145728
  (1 shorter events, 0.0 us)

commit v4 on v3

--- a/solution.py
+++ b/solution.py
@@ -309,9 +309,8 @@
             return carry
 
         per_chunk = chunk // pad
-        relay_part = near_steps // per_chunk
         for part in range(rows // chunk):
-            if part == relay_part:
+            if part == 0:
 
                 @pl.when(relays)
                 def _():

time: 115 us -> 112 us (0.974)
  Pallas kernels: 109 us -> 107 us
    pallas_call x1, Pallas kernels: 109 us -> 107 us  [both_steps(): pl.pallas_call(functools.partial(steps_kernel, bands, sectors), out_shape...]
where the time goes in v4:
time: 112 us
  Pallas kernels  107 us (96%)
  local copies, waits for them, and re-layouts  3.49 us (3%)
  other arithmetic  2.1 us (2%)
    pallas_call x1, Pallas kernels, both_steps(): pl.pallas_call(functools.partial(steps_kernel, bands, sectors), out_shape...  107 us
    unnamed x1, local copies, waits for them, and re-layouts  2.67 us

profile of v4, /device:TPU:5, one launch (start us, length us, event | category | flops | bytes accessed | tf_op | source)
XLA Modules:
  0.0 112.2 jit_solution(636106748145470717)
XLA Ops:
  0.0 0.7 fusion
  0.7 1.3 %copy_bitcast_fusion = (s32[2,288]{1,0:T(2,128)}, s32[2,288]{1,0:T(2,128)}) fusion(s32[2,1,288]{2,1,0:T(1,128)} %targets_ref.1, s32[2,1,288]{2,1,0:T(1,128)} %param.13, s32[2,1,288]{2,1,0:T(1,128)} %param.12), kind=kLoop, calls=%fused_computation.3 | loop fusion | flops 1152 | bytes 11520
  2.1 0.1 squeeze.18
  2.1 0.1 squeeze.19
  2.2 0.1 pad_add_fusion
  2.3 0.6 pad.4
  2.9 106.5 %both_steps.1 = f32[96,32,128]{2,1,0:T(8,128)} custom-call(s32[2,288]{1,0:T(2,128)} %get-tuple-element.8.own_ref, s32[2,288]{1,0:T(2,128)} %get-tuple-element.7.far_tgt_ref, s32[2,1,288]{2,1,0:T(1,128)} %own_src_ref.1, s32[24,1,128]{2,1,0:T(1,128)} %bitcast.9, s32[2,1,288]{2,1,0:T(1,128)} %targets_ref.1, bf16[96,32,128]{2,1,0:T(8,128)(2,1)} %bitcast.8, ...), custom_call_target="tpu_custom_call" | custom-call | flops 1207959552 | bytes 37748736 | tf_op jit(solution)/shard_map/both_steps/pallas_call | solution.py:388
  109.5 2.7 %copy.34 = f32[1,96,32,128]{3,2,1,0:T(8,128)} copy(f32[1,96,32,128]{3,2,1,0:T(8,128)} %bitcast.7) | data formatting | bytes 3145728
  (1 shorter events, 0.0 us)
